TPU v7x, 32 devices: a whole 2x2x4 slice. The times are simulated.
32 devices in a mesh: prow: 16 (over z, y, core), pcol: 2 (over x).
Axes of the slice: x: 2, y: 2, z: 4, core: 2. Of those that a mesh axis runs over, the one named last changes fastest.
Arguments:
- prior_panel: bfloat16 [16384, 12288], P('prow', 'pcol'), may hold values from -0.0546875 to 0.0546875
- prior_solution: bfloat16 [12288, 256], P('pcol', 'prow'), may hold values from -6 to 6
- right_side: bfloat16 [16384, 256], P('prow', 'pcol'), may hold values from -6 to 6
- new_panel: bfloat16 [2, 16384, 512], P(None, 'prow', 'pcol'), may hold values from -0.25 to 0.25
- inverses: bfloat16 [2, 512, 512], P(None, 'pcol'), as said below
Outputs:
- solved: bfloat16 [2, 512, 256], P(None, 'pcol')
- pending: float32 [16384, 256], P('prow', 'pcol')
Inputs may be any that keep to these rules, and one draw needn't show every extreme that they name: `inverses`: each of the two inverse blocks is lower triangular with a positive diagonal.
All inputs are finite; a program needn't handle non-finite values.
Results may differ from a plain program's by a relative error of at most 0.0057.
Values may be sent and summed in bfloat16 or wider, within the bound.
A program may use at most 64 MiB of HBM per device.

v0:
```python
import jax
import jax.numpy as jnp
from jax import lax
from jax.sharding import PartitionSpec as P


def spread(block, axis, owner):
    block = jnp.where(lax.axis_index(axis) == owner, block, jnp.zeros_like(block))
    return lax.psum(block, axis)


def body(prior_panel, prior_solution, right_side, new_panel, inverses):
    local_rows = prior_panel.shape[0]
    block_size = inverses.shape[2]
    pair_rows = 2 * block_size
    partial_value = jnp.dot(
        prior_panel,
        lax.all_gather(prior_solution, "prow", axis=1, tiled=True),
        preferred_element_type=jnp.float32,
    )
    row_ids = lax.axis_index("prow") * local_rows + lax.iota(jnp.int32, local_rows)
    first_panel = jnp.where(
        (row_ids >= block_size)[:, None], new_panel[0], jnp.zeros_like(new_panel[0])
    )
    second_panel = jnp.where(
        (row_ids >= pair_rows)[:, None], new_panel[1], jnp.zeros_like(new_panel[1])
    )
    pending = right_side.astype(jnp.float32) - lax.psum_scatter(
        partial_value, "pcol", scatter_dimension=1, tiled=True
    )
    solved_list = []
    for section, masked in ((0, first_panel), (1, second_panel)):
        diagonal = pending[section * block_size : (section + 1) * block_size].astype(jnp.bfloat16)
        gathered = lax.all_gather(diagonal, "pcol", axis=1, tiled=True)
        result = spread(
            jnp.dot(inverses[section], gathered, preferred_element_type=jnp.float32).astype(
                jnp.bfloat16
            ),
            "prow",
            0,
        )
        update = jnp.dot(masked, result, preferred_element_type=jnp.float32)
        pending = pending - lax.psum_scatter(update, "pcol", scatter_dimension=1, tiled=True)
        solved_list.append(result)
    first_x = solved_list[0]
    second_x = solved_list[1]
    return (jnp.stack([first_x, second_x]), pending)


def solution(mesh):
    return jax.shard_map(
        body,
        mesh=mesh,
        in_specs=(
            P("prow", "pcol"),
            P("pcol", "prow"),
            P("prow", "pcol"),
            P(None, "prow", "pcol"),
            P(None, "pcol", None),
        ),
        out_specs=(P(None, "pcol", None), P("prow", "pcol")),
        check_vma=False,
    )
```

profile of v0, /device:TPU:0, one launch (start us, length us, event | category | flops | bytes accessed | tf_op | source)
XLA Modules:
  0.0 335.1 jit_solution(1964586816087864626)
XLA Ops:
  7.2 0.7 all-gather.2.cloned.1.call-update
  7.9 0.0 reduce-scatter.4.cloned.1.call-start
  8.0 50.2 %all-gather.2.cloned.1.call-done = bf16[6144,256]{0,1:T(8,128)(2,1)} async-done(((bf16[6144,16]{0,1:T(8,128)(2,1)}), bf16[6144,256]{0,1:T(8,128)(2,1)}) %all-gather.2.cloned.1.call-update) | async-done | bytes 3145744 | tf_op jit(solution)/shard_map/all_gather | solution.py:18
  58.2 9.9 %fusion.20 = f32[1024,256]{1,0:T(8,128)} fusion(bf16[1024,6144]{1,0:T(8,128)(2,1)} %param.5, bf16[6144,256]{0,1:T(8,128)(2,1)} %all-gather.2.cloned.1.call-done), kind=kOutput, calls=%fused_computation.29 | convolution fusion | flops 3221225472 | bytes 16777216 | tf_op jit(solution)/shard_map/dot_general | solution.py:16
  68.2 0.0 all-reduce.3.cloned.1.call-start
  68.2 19.2 %reduce-scatter.4.cloned.1.call-done = f32[1024,128]{1,0:T(8,128)} async-done(((f32[1024,256]{1,0:T(8,128)}), f32[1024,128]{1,0:T(8,128)}) %reduce-scatter.4.cloned.1.call-update) | async-done | bytes 524304 | tf_op jit(solution)/shard_map/reduce_scatter | solution.py:28
  87.4 1.1 convert_subtract_fusion
  88.5 5.9 %all_gather.10 = bf16[512,256]{1,0:T(8,128)(2,1)S(1)} all-gather(bf16[512,128]{1,0:T(8,128)(2,1)S(1)} %slice.47), channel_id=1, replica_groups=mesh['prow'=16,'pcol'=2] {'pcol'}, dimensions={1}, use_global_device_ids=true | all-gather | bytes 393216 | tf_op jit(solution)/shard_map/all_gather | solution.py:34
  94.5 0.9 fusion.1
  95.4 0.0 reduce-scatter.6.cloned.1.call-start
  95.5 87.0 %all-reduce.3.cloned.1.call-done = bf16[256,256]{0,1:T(8,128)(2,1)} async-done(((bf16[256,256]{0,1:T(8,128)(2,1)}), bf16[256,256]{0,1:T(8,128)(2,1)}) %all-reduce.3.cloned.1.call-update) | async-done | bytes 131088 | tf_op jit(solution)/shard_map/psum | solution.py:9
  182.6 2.2 fusion.5
  184.8 0.0 all-reduce.5.cloned.1.call-start
  184.9 22.0 %reduce-scatter.6.cloned.1.call-done = f32[1024,128]{1,0:T(8,128)} async-done(((f32[1024,256]{1,0:T(8,128)}), f32[1024,128]{1,0:T(8,128)}) %reduce-scatter.6.cloned.1.call-update) | async-done | bytes 524304 | tf_op jit(solution)/shard_map/reduce_scatter | solution.py:43
  206.9 1.1 sub.10
  208.0 6.0 %all_gather.11 = bf16[512,256]{1,0:T(8,128)(2,1)S(1)} all-gather(bf16[512,128]{1,0:T(8,128)(2,1)S(1)} %slice.46), channel_id=1, replica_groups=mesh['prow'=16,'pcol'=2] {'pcol'}, dimensions={1}, use_global_device_ids=true | all-gather | bytes 393216 | tf_op jit(solution)/shard_map/all_gather | solution.py:34
  214.0 0.9 fusion.3
  215.0 0.0 reduce-scatter.8.cloned.1.call-start
  215.0 87.0 %all-reduce.5.cloned.1.call-done = bf16[256,256]{0,1:T(8,128)(2,1)} async-done(((bf16[256,256]{0,1:T(8,128)(2,1)}), bf16[256,256]{0,1:T(8,128)(2,1)}) %all-reduce.5.cloned.1.call-update) | async-done | bytes 131088 | tf_op jit(solution)/shard_map/psum | solution.py:9
  302.0 2.2 fusion.4
  304.3 1.0 pad_maximum_fusion
  305.3 0.8 copy.7
  306.1 20.3 %reduce-scatter.8.cloned.1.call-done = f32[1024,128]{1,0:T(8,128)} async-done(((f32[1024,256]{1,0:T(8,128)}), f32[1024,128]{1,0:T(8,128)}) %reduce-scatter.8.cloned.1.call-update) | async-done | bytes 524304 | tf_op jit(solution)/shard_map/reduce_scatter | solution.py:43
  326.4 1.9 sub.11
  (16 shorter events, 0.2 us)
Async XLA Ops:
  7.2 80.3 %copy-start.1 = (bf16[1024,128]{1,0:T(8,128)(2,1)S(1)}, bf16[1024,128]{1,0:T(8,128)(2,1)}, u32[]{:S(2)}) copy-start(bf16[1024,128]{1,0:T(8,128)(2,1)} %param.7) | copy-start | bytes 786436
  7.2 51.0 %all-gather.2.cloned.1.call-start = ((), (), s32[]{:S(2)}) async-start(), calls=%async_computation.3 | async-start | bytes 3342336 | tf_op jit(solution)/shard_map/all_gather | solution.py:18
  7.9 86.6 %copy-start.2 = (bf16[2,256,512]{2,1,0:T(8,128)(2,1)S(1)}, bf16[2,256,512]{2,1,0:T(8,128)(2,1)}, u32[]{:S(2)}) copy-start(bf16[2,256,512]{2,1,0:T(8,128)(2,1)} %param.9) | copy-start | bytes 1572868
  7.9 174.6 %copy-start = (bf16[2,1024,256]{2,1,0:T(8,128)(2,1)S(1)}, bf16[2,1024,256]{2,1,0:T(8,128)(2,1)}, u32[]{:S(2)}) copy-start(bf16[2,1024,256]{2,1,0:T(8,128)(2,1)} %param.8) | copy-start | bytes 3145732
  7.9 79.5 %reduce-scatter.4.cloned.1.call-start = ((), (), s32[]{:S(2)}) async-start(), calls=%async_computation.4 | async-start | bytes 1572864 | tf_op jit(solution)/shard_map/reduce_scatter | solution.py:28
  68.2 114.4 %all-reduce.3.cloned.1.call-start = ((), (), s32[]{:S(2)}) async-start(), calls=%async_computation.5 | async-start | bytes 262144 | tf_op jit(solution)/shard_map/psum | solution.py:9
  95.4 111.5 %reduce-scatter.6.cloned.1.call-start = ((), (), s32[]{:S(2)}) async-start(), calls=%async_computation.6 | async-start | bytes 1572864 | tf_op jit(solution)/shard_map/reduce_scatter | solution.py:43
  184.8 117.2 %all-reduce.5.cloned.1.call-start = ((), (), s32[]{:S(2)}) async-start(), calls=%async_computation.7 | async-start | bytes 262144 | tf_op jit(solution)/shard_map/psum | solution.py:9
  215.0 111.4 %reduce-scatter.8.cloned.1.call-start = ((), (), s32[]{:S(2)}) async-start(), calls=%async_computation.8 | async-start | bytes 1572864 | tf_op jit(solution)/shard_map/reduce_scatter | solution.py:43
Sparse Core Ops, SparseCore 0:
  10.3 47.8 all-gather.1
  68.3 19.1 reduce-scatter.3
  95.6 86.9 all-reduce.2
  184.9 21.9 reduce-scatter.5
  215.1 86.9 all-reduce.4
  304.4 21.9 reduce-scatter.7
where the time goes:
time: 335 us
  waiting for transfers between devices  287 us (86%)
  matrix products  16.2 us (5%)
  between operations  14.2 us (4%)
  blocking collectives  11.9 us (4%)
  other arithmetic  5.08 us (2%)
    psum x2, waiting for transfers between devices, spread(): return lax.psum(block, axis)  174 us
    all_gather x1, waiting for transfers between devices, body(): lax.all_gather(prior_solution, 'prow', axis=1, tiled=True)  50.2 us
    reduce_scatter x2, waiting for transfers between devices, body(): lax.psum_scatter(update, 'pcol', scatter_dimension=1, tiled=True)  42.3 us
    reduce_scatter x1, waiting for transfers between devices, body(): lax.psum_scatter(partial_value, 'pcol', scatter_dimension=1, tiled=True)  19.2 us
    all_gather x2, blocking collectives, body(): gathered = lax.all_gather(diagonal, 'pcol', axis=1, tiled=True)  11.9 us
    dot_general x1, matrix products, body(): jnp.dot(prior_panel, lax.all_gather(prior_solution, 'prow', axis=1, tiled...  9.91 us
  transfers between devices with their start and end apart: 6, of which 6 were waited for; matrix products, arithmetic and copies ran while one was open for 1% of the time, Pallas kernels for 0%

commit v1 on v0

--- a/solution.py
+++ b/solution.py
@@ -6,7 +6,11 @@
 
 def spread(block, axis, owner):
     block = jnp.where(lax.axis_index(axis) == owner, block, jnp.zeros_like(block))
-    return lax.psum(block, axis)
+
+    def tell_stocks_over_axis(a0, link_axis):
+        return jnp.sum(lax.all_gather(a0, link_axis), axis=0)
+
+    return tell_stocks_over_axis(block, axis)
 
 
 def body(prior_panel, prior_solution, right_side, new_panel, inverses):

time: 335 us -> 244 us (0.73)
  waiting for transfers between devices: 287 us -> 191 us
  local copies, waits for them, and re-layouts: 0.89 us -> 5.43 us
    psum x2 -> x0, waiting for transfers between devices: 174 us -> none  [spread(): return lax.psum(block, axis)]
    all_gather x0 -> x2, waiting for transfers between devices: none -> 82.6 us  [tell_stocks_over_axis(): return jnp.sum(lax.all_gather(a0, link_axis), axis=0)]
    unnamed x7 -> x9, local copies, waits for them, and re-layouts: 0.85 us -> 5.4 us
    reduce_scatter x2, waiting for transfers between devices: 42.3 us -> 37.8 us  [body(): lax.psum_scatter(update, 'pcol', scatter_dimension=1, tiled=True)]
  transfers between devices with their start and end apart: 6 -> 6, of which waited for: 6 -> 6; matrix products, arithmetic and copies ran while one was open for 1% -> 0% of each run, Pallas kernels for 0% -> 0%
where the time goes in v1:
time: 244 us; the launch traced here: 243 us
  waiting for transfers between devices  191 us (78%)
  matrix products  14.4 us (6%)
  between operations  14.2 us (6%)
  blocking collectives  11.9 us (5%)
  other arithmetic  6.43 us (3%)
  local copies, waits for them, and re-layouts  5.43 us (2%)
    all_gather x2, waiting for transfers between devices, tell_stocks_over_axis(): return jnp.sum(lax.all_gather(a0, link_axis), axis=0)  82.6 us
    all_gather x1, waiting for transfers between devices, body(): lax.all_gather(prior_solution, 'prow', axis=1, tiled=True)  50.2 us
    reduce_scatter x2, waiting for transfers between devices, body(): lax.psum_scatter(update, 'pcol', scatter_dimension=1, tiled=True)  37.8 us
    reduce_scatter x1, waiting for transfers between devices, body(): lax.psum_scatter(partial_value, 'pcol', scatter_dimension=1, tiled=True)  19.2 us
    all_gather x2, blocking collectives, body(): gathered = lax.all_gather(diagonal, 'pcol', axis=1, tiled=True)  11.9 us
    dot_general x1, matrix products, body(): jnp.dot(prior_panel, lax.all_gather(prior_solution, 'prow', axis=1, tiled...  9.91 us
    unnamed x9, local copies, waits for them, and re-layouts  5.4 us
  transfers between devices with their start and end apart: 6, of which 6 were waited for; matrix products, arithmetic and copies ran while one was open for 0% of the time, Pallas kernels for 0%

profile of v1, /device:TPU:0, one launch (start us, length us, event | category | flops | bytes accessed | tf_op | source)
XLA Modules:
  0.0 243.3 jit_solution(13464831863398649971)
XLA Ops:
  7.2 0.7 all-gather.6.cloned.1.call-update
  8.0 50.2 %all-gather.6.cloned.1.call-done = bf16[6144,256]{0,1:T(8,128)(2,1)} async-done(((bf16[6144,16]{0,1:T(8,128)(2,1)}), bf16[6144,256]{0,1:T(8,128)(2,1)}) %all-gather.6.cloned.1.call-update) | async-done | bytes 3145744 | tf_op jit(solution)/shard_map/all_gather | solution.py:22
  58.2 9.9 %fusion.20 = f32[1024,256]{1,0:T(8,128)} fusion(bf16[1024,6144]{1,0:T(8,128)(2,1)} %param.5, bf16[6144,256]{0,1:T(8,128)(2,1)} %all-gather.6.cloned.1.call-done), kind=kOutput, calls=%fused_computation.31 | convolution fusion | flops 3221225472 | bytes 16777216 | tf_op jit(solution)/shard_map/dot_general | solution.py:20
  68.1 0.0 all-gather.8.cloned.1.call-start
  68.2 19.2 %reduce-scatter.4.cloned.1.call-done = f32[1024,128]{1,0:T(8,128)} async-done(((f32[1024,256]{1,0:T(8,128)}), f32[1024,128]{1,0:T(8,128)}) %reduce-scatter.4.cloned.1.call-update) | async-done | bytes 524304 | tf_op jit(solution)/shard_map/reduce_scatter | solution.py:32
  87.4 1.1 convert_subtract_fusion
  88.5 6.0 %all_gather.22 = bf16[512,256]{1,0:T(8,128)(2,1)S(1)} all-gather(bf16[512,128]{1,0:T(8,128)(2,1)S(1)} %slice.47), channel_id=1, replica_groups=mesh['prow'=16,'pcol'=2] {'pcol'}, dimensions={1}, use_global_device_ids=true | all-gather | bytes 393216 | tf_op jit(solution)/shard_map/all_gather | solution.py:38
  94.5 0.9 fusion.1
  95.4 0.0 reduce-scatter.6.cloned.1.call-start
  95.5 41.3 %all-gather.8.cloned.1.call-done = bf16[4096,256]{0,1:T(8,128)(2,1)} async-done(((bf16[256,256]{0,1:T(8,128)(2,1)}), bf16[4096,256]{0,1:T(8,128)(2,1)}) %all-gather.8.cloned.1.call-update) | async-done | bytes 2097168 | tf_op jit(solution)/shard_map/all_gather | solution.py:11
  136.8 2.3 copy.8
  139.1 1.2 bitcast_reduce_fusion.1
  140.3 1.3 fusion.5
  141.7 19.3 %reduce-scatter.6.cloned.1.call-done = f32[1024,128]{1,0:T(8,128)} async-done(((f32[1024,256]{1,0:T(8,128)}), f32[1024,128]{1,0:T(8,128)}) %reduce-scatter.6.cloned.1.call-update) | async-done | bytes 524304 | tf_op jit(solution)/shard_map/reduce_scatter | solution.py:47
  161.1 1.1 sub.10
  162.2 6.0 %all_gather.25 = bf16[512,256]{1,0:T(8,128)(2,1)S(1)} all-gather(bf16[512,128]{1,0:T(8,128)(2,1)S(1)} %slice.46), channel_id=1, replica_groups=mesh['prow'=16,'pcol'=2] {'pcol'}, dimensions={1}, use_global_device_ids=true | all-gather | bytes 393216 | tf_op jit(solution)/shard_map/all_gather | solution.py:38
  168.1 0.9 fusion.3
  169.2 41.3 %all-gather.10.cloned.1.call-done = bf16[4096,256]{0,1:T(8,128)(2,1)} async-done(((bf16[256,256]{0,1:T(8,128)(2,1)}), bf16[4096,256]{0,1:T(8,128)(2,1)}) %all-gather.10.cloned.1.call-update) | async-done | bytes 2097168 | tf_op jit(solution)/shard_map/all_gather | solution.py:11
  210.5 2.2 copy.9
  212.7 1.2 bitcast_reduce_fusion
  213.9 1.3 fusion.4
  215.3 0.8 copy.7
  216.1 18.5 %reduce-scatter.8.cloned.1.call-done = f32[1024,128]{1,0:T(8,128)} async-done(((f32[1024,256]{1,0:T(8,128)}), f32[1024,128]{1,0:T(8,128)}) %reduce-scatter.8.cloned.1.call-update) | async-done | bytes 524304 | tf_op jit(solution)/shard_map/reduce_scatter | solution.py:47
  234.6 1.9 sub.11
  (20 shorter events, 0.3 us)
Async XLA Ops:
  7.2 51.0 %all-gather.6.cloned.1.call-start = ((), (), s32[]{:S(2)}) async-start(), calls=%async_computation.3 | async-start | bytes 3342336 | tf_op jit(solution)/shard_map/all_gather | solution.py:22
  7.9 79.5 %copy-start.1 = (bf16[1024,128]{1,0:T(8,128)(2,1)S(1)}, bf16[1024,128]{1,0:T(8,128)(2,1)}, u32[]{:S(2)}) copy-start(bf16[1024,128]{1,0:T(8,128)(2,1)} %param.7) | copy-start | bytes 786436
  7.9 86.6 %copy-start.2 = (bf16[2,256,512]{2,1,0:T(8,128)(2,1)S(1)}, bf16[2,256,512]{2,1,0:T(8,128)(2,1)}, u32[]{:S(2)}) copy-start(bf16[2,256,512]{2,1,0:T(8,128)(2,1)} %param.9) | copy-start | bytes 1572868
  7.9 79.5 %reduce-scatter.4.cloned.1.call-start = ((), (), s32[]{:S(2)}) async-start(), calls=%async_computation.4 | async-start | bytes 1572864 | tf_op jit(solution)/shard_map/reduce_scatter | solution.py:32
  68.1 68.7 %all-gather.8.cloned.1.call-start = ((), (), s32[]{:S(2)}) async-start(), calls=%async_computation.7 | async-start | bytes 2228224 | tf_op jit(solution)/shard_map/all_gather | solution.py:11
  95.4 65.6 %reduce-scatter.6.cloned.1.call-start = ((), (), s32[]{:S(2)}) async-start(), calls=%async_computation.5 | async-start | bytes 1572864 | tf_op jit(solution)/shard_map/reduce_scatter | solution.py:47
  136.8 3.5 %copy-start = (bf16[2,1024,256]{2,1,0:T(8,128)(2,1)S(1)}, bf16[2,1024,256]{2,1,0:T(8,128)(2,1)}, u32[]{:S(2)}) copy-start(bf16[2,1024,256]{2,1,0:T(8,128)(2,1)} %param.8) | copy-start | bytes 3145732
  141.7 68.8 %all-gather.10.cloned.1.call-start = ((), (), s32[]{:S(2)}) async-start(), calls=%async_computation.8 | async-start | bytes 2228224 | tf_op jit(solution)/shard_map/all_gather | solution.py:11
  169.1 65.5 %reduce-scatter.8.cloned.1.call-start = ((), (), s32[]{:S(2)}) async-start(), calls=%async_computation.6 | async-start | bytes 1572864 | tf_op jit(solution)/shard_map/reduce_scatter | solution.py:47
Sparse Core Ops, SparseCore 0:
  10.3 47.8 all-gather.5
  68.3 19.1 reduce-scatter.3
  95.6 41.1 all-gather.7
  141.8 19.2 reduce-scatter.5
  169.2 41.1 all-gather.9
  215.3 19.2 reduce-scatter.7
